TPU v7x, 32 devices: a whole 2x2x4 slice. The times are simulated.
32 devices in a mesh: grp: 4 (over y, core), dev: 8 (over z, x).
Axes of the slice: x: 2, y: 2, z: 4, core: 2. Of those that a mesh axis runs over, the one named last changes fastest.
Arguments:
- queries: bfloat16 [3072, 1024], P('dev'), may hold values from -16 to 16
- docs: bfloat16 [4096, 1024], P(('grp', 'dev')), may hold values from -16 to 16
- compat: int32 [24, 32], P('dev', 'grp'), may hold values from 0 to 1, as said below
- positives: int32 [3072], P('dev'), may hold values from 0 to 4095, as said below
Outputs:
- loss: float32 [3072], P('dev')
- query_grad: float32 [3072, 1024], P('dev')
- doc_grad: float32 [4096, 1024], P(('grp', 'dev'))
Inputs may be any that keep to these rules, and one draw needn't show every extreme that they name: compat[b, b % 32] is 1 for every query block b. positives[i] lies in a document block that is compatible with the block of query i.
All inputs are finite; a program needn't handle non-finite values.
Results may differ from a plain program's by a relative error of at most 0.0007.
Values may be sent and summed in bfloat16 or wider, within the bound.
A program may use at most 128 MiB of HBM per device.

v0:
```python
import jax
import jax.numpy as jnp
from jax import lax
from jax.sharding import PartitionSpec as P

BLOCK = 128
LOGIT_SCALE = 0.1
NEG_FLOOR = -1e30


def joined(value, axis, combine):
    everything = jax.tree.map(lambda part: lax.all_gather(part, axis), value)
    first = jax.tree.map(lambda part: part[0], everything)

    def hop(k, so_far):
        return combine(so_far, jax.tree.map(lambda part: part[k], everything))

    return lax.fori_loop(1, lax.axis_size(axis), hop, first)


def from_behind(value, axis, by):
    devices = lax.axis_size(axis)
    return lax.ppermute(value, axis, [(i, (i + by) % devices) for i in range(devices)])


def panel_scores(queries, panel):
    return LOGIT_SCALE * lax.dot_general(
        queries, panel, (((1,), (1,)), ((), ())), preferred_element_type=jnp.float32
    )


def panel_masks(compat, positives, column_start, doc_offset, block, panel_rows):
    blocks = lax.dynamic_slice_in_dim(compat, column_start, panel_rows // block, 1)
    live = jnp.repeat(jnp.repeat(blocks, block, axis=0), block, axis=1) > 0
    doc_ids = doc_offset + jnp.arange(panel_rows, dtype=jnp.int32)
    target = doc_ids[None, :] == positives[:, None]
    return (live, target)


def add_stats(stats, scores, live, target):
    row_max, total, chosen = stats
    local_max = jnp.max(jnp.where(live, scores, NEG_FLOOR), axis=1)
    new_max = jnp.maximum(row_max, local_max)
    terms = jnp.where(live, jnp.exp(scores - new_max[:, None]), 0.0)
    total = total * jnp.exp(row_max - new_max) + jnp.sum(terms, axis=1)
    chosen = chosen + jnp.sum(jnp.where(target, scores, 0.0), axis=1)
    return (new_max, total, chosen)


def merge_stats(first, second):
    top = jnp.maximum(first[0], second[0])
    total = first[1] * jnp.exp(first[0] - top) + second[1] * jnp.exp(second[0] - top)
    return (top, total, first[2] + second[2])


def finish_stats(stats):
    row_max, total, chosen = joined(stats, "grp", merge_stats)
    lse = row_max + jnp.log(total)
    return (lse, lse - chosen)


def coefficients(scores, live, target, lse):
    prob = jnp.where(live, jnp.exp(scores - lse[:, None]), 0.0)
    return (prob - target.astype(jnp.float32)).astype(jnp.bfloat16)


def local(queries, docs, compat, positives):
    width = lax.axis_size("dev")
    position = lax.axis_index("dev")
    group_index = lax.axis_index("grp")
    block = BLOCK
    panel_rows = docs.shape[0]
    query_rows = queries.shape[0]
    panel_blocks = panel_rows // block
    group_start = group_index * (width * panel_rows)
    empty_stats = (
        jnp.full((query_rows,), NEG_FLOOR, jnp.float32),
        jnp.zeros((query_rows,), jnp.float32),
        jnp.zeros((query_rows,), jnp.float32),
    )

    def masks_for(owner):
        return panel_masks(
            compat,
            positives,
            owner * panel_blocks,
            group_start + owner * panel_rows,
            block,
            panel_rows,
        )

    def visit(stats, panel, owner):
        live, target = masks_for(owner)
        scores = panel_scores(queries, panel)
        return (add_stats(stats, scores, live, target), scores)

    def gradient_step(carry, panel, scores, owner, lse):
        live, target = masks_for(owner)
        query_sum, doc_sum = carry
        coef = coefficients(scores, live, target, lse)
        query_sum = query_sum + LOGIT_SCALE * jnp.dot(
            coef, panel, preferred_element_type=jnp.float32
        )
        doc_sum = doc_sum + LOGIT_SCALE * lax.dot_general(
            coef, queries, (((0,), (0,)), ((), ())), preferred_element_type=jnp.float32
        )
        return (query_sum, doc_sum)

    stats, first_scores = visit(empty_stats, docs, position)
    store = jnp.zeros((width,) + docs.shape, docs.dtype).at[0].set(docs)
    score_store = jnp.zeros((width, query_rows, panel_rows), jnp.float32).at[0].set(first_scores)

    def first_turn(turn_index, carry):
        current, kept, kept_scores, partial_value = carry
        current = from_behind(current, "dev", 1)
        owner = (position - turn_index) % width
        kept = lax.dynamic_update_index_in_dim(kept, current, turn_index, 0)
        partial_value, scores = visit(partial_value, current, owner)
        kept_scores = lax.dynamic_update_index_in_dim(kept_scores, scores, turn_index, 0)
        return (current, kept, kept_scores, partial_value)

    current, store, score_store, stats = lax.fori_loop(
        1, width, first_turn, (docs, store, score_store, stats)
    )
    lse, loss = finish_stats(stats)
    start_carry = (
        jnp.zeros((query_rows, docs.shape[1]), jnp.float32),
        jnp.zeros((panel_rows, docs.shape[1]), jnp.float32),
    )
    start_carry = gradient_step(start_carry, docs, score_store[0], position, lse)

    def second_turn(turn_index, carry):
        query_sum, doc_sum = carry
        doc_sum = from_behind(doc_sum, "dev", 1)
        owner = (position - turn_index) % width
        panel = lax.dynamic_index_in_dim(store, turn_index, 0, keepdims=False)
        scores = lax.dynamic_index_in_dim(score_store, turn_index, 0, keepdims=False)
        return gradient_step((query_sum, doc_sum), panel, scores, owner, lse)

    query_part, doc_part = lax.fori_loop(1, width, second_turn, start_carry)
    doc_grad = from_behind(doc_part, "dev", 1)
    query_grad = lax.psum(query_part, "grp")
    return (loss, query_grad, doc_grad)


def solution(mesh):
    return jax.shard_map(
        local,
        mesh=mesh,
        in_specs=(P("dev", None), P(("grp", "dev"), None), P("dev", "grp"), P("dev")),
        out_specs=(P("dev"), P("dev", None), P(("grp", "dev"), None)),
        check_vma=False,
    )
```

profile of v0, /device:TPU:0, one launch (start us, length us, event | category | flops | bytes accessed | tf_op | source)
XLA Modules:
  0.0 280.5 jit_solution(13684167352823001613)
XLA Ops:
  14.8 83.8 %while.67 = (s32[]{:T(128)}, bf16[128,1024]{1,0:T(8,128)(2,1)}, bf16[8,128,1024]{2,1,0:T(8,128)(2,1)S(1)}, f32[8,384,128]{1,2,0:T(8,128)}, f32[384]{0:T(512)S(1)...) while((s32[]{:T(128)}, bf16[128,1024]{1,0:T(8,128)(2,1)}, ...), condition=%wide.region_7.8_spmd, body=%wide.region_3.7_spmd.sunk | while | flops 101106560 | bytes 3962444 | solution.py:122
  14.8 2.9 %collective-permute-start = (bf16[128,1024]{1,0:T(8,128)(2,1)}, bf16[128,1024]{1,0:T(8,128)(2,1)S(1)}, u32[]{:S(2)}, u32[]{:S(2)}) collective-permute-start(bf16[128,1024]{1,0:T(8,128)(2,1)} %get-tuple-element.1277), channel_id=1, source_target_pairs={{0,1},{1,2},{2,3},{3,4},{4,5},{5,6},{6,7},{7,0},{8,9},{9,10},{10,1... | collective-permute-start | bytes 786440 | tf_op jit(solution)/shard_map/while/body/eval_jaxpr/ppermute | solution.py:23
  17.8 9.5 %collective-permute-done = bf16[128,1024]{1,0:T(8,128)(2,1)S(1)} collective-permute-done((bf16[128,1024]{1,0:T(8,128)(2,1)}, bf16[128,1024]{1,0:T(8,128)(2,1)S(1)}, u32[]{:S(2)}, u32[]{:S(2)}) %collective-permute-start) | collective-permute-done | bytes 262176 | tf_op jit(solution)/shard_map/while/body/eval_jaxpr/ppermute | solution.py:23
  29.5 10.2 %collective-permute-done = bf16[128,1024]{1,0:T(8,128)(2,1)S(1)} collective-permute-done((bf16[128,1024]{1,0:T(8,128)(2,1)}, bf16[128,1024]{1,0:T(8,128)(2,1)S(1)}, u32[]{:S(2)}, u32[]{:S(2)}) %collective-permute-start) | collective-permute-done | bytes 262176 | tf_op jit(solution)/shard_map/while/body/eval_jaxpr/ppermute | solution.py:23
  41.9 9.3 %collective-permute-done = bf16[128,1024]{1,0:T(8,128)(2,1)S(1)} collective-permute-done((bf16[128,1024]{1,0:T(8,128)(2,1)}, bf16[128,1024]{1,0:T(8,128)(2,1)S(1)}, u32[]{:S(2)}, u32[]{:S(2)}) %collective-permute-start) | collective-permute-done | bytes 262176 | tf_op jit(solution)/shard_map/while/body/eval_jaxpr/ppermute | solution.py:23
  53.4 9.1 %collective-permute-done = bf16[128,1024]{1,0:T(8,128)(2,1)S(1)} collective-permute-done((bf16[128,1024]{1,0:T(8,128)(2,1)}, bf16[128,1024]{1,0:T(8,128)(2,1)S(1)}, u32[]{:S(2)}, u32[]{:S(2)}) %collective-permute-start) | collective-permute-done | bytes 262176 | tf_op jit(solution)/shard_map/while/body/eval_jaxpr/ppermute | solution.py:23
  64.8 9.1 %collective-permute-done = bf16[128,1024]{1,0:T(8,128)(2,1)S(1)} collective-permute-done((bf16[128,1024]{1,0:T(8,128)(2,1)}, bf16[128,1024]{1,0:T(8,128)(2,1)S(1)}, u32[]{:S(2)}, u32[]{:S(2)}) %collective-permute-start) | collective-permute-done | bytes 262176 | tf_op jit(solution)/shard_map/while/body/eval_jaxpr/ppermute | solution.py:23
  76.1 9.1 %collective-permute-done = bf16[128,1024]{1,0:T(8,128)(2,1)S(1)} collective-permute-done((bf16[128,1024]{1,0:T(8,128)(2,1)}, bf16[128,1024]{1,0:T(8,128)(2,1)S(1)}, u32[]{:S(2)}, u32[]{:S(2)}) %collective-permute-start) | collective-permute-done | bytes 262176 | tf_op jit(solution)/shard_map/while/body/eval_jaxpr/ppermute | solution.py:23
  87.4 9.1 %collective-permute-done = bf16[128,1024]{1,0:T(8,128)(2,1)S(1)} collective-permute-done((bf16[128,1024]{1,0:T(8,128)(2,1)}, bf16[128,1024]{1,0:T(8,128)(2,1)S(1)}, u32[]{:S(2)}, u32[]{:S(2)}) %collective-permute-start) | collective-permute-done | bytes 262176 | tf_op jit(solution)/shard_map/while/body/eval_jaxpr/ppermute | solution.py:23
  98.5 5.2 %all-gather.5 = f32[4,1,384]{2,1,0:T(1,128)S(1)} all-gather(f32[1,1,384]{2,1,0:T(1,128)S(1)} %reshape.269), channel_id=4, replica_groups=mesh['grp'=4,'dev'=8] {'grp'}, dimensions={0}, use_global_device_ids=true | all-gather | bytes 7680 | tf_op jit(solution)/shard_map/all_gather | solution.py:12
  103.7 5.2 %all-gather.4 = f32[4,1,384]{2,1,0:T(1,128)S(1)} all-gather(f32[1,1,384]{2,1,0:T(1,128)S(1)} %reshape.267), channel_id=3, replica_groups=mesh['grp'=4,'dev'=8] {'grp'}, dimensions={0}, use_global_device_ids=true | all-gather | bytes 7680 | tf_op jit(solution)/shard_map/all_gather | solution.py:12
  108.9 5.2 %all-gather.3 = f32[4,1,384]{2,1,0:T(1,128)S(1)} all-gather(f32[1,1,384]{2,1,0:T(1,128)S(1)} %reshape.265), channel_id=2, replica_groups=mesh['grp'=4,'dev'=8] {'grp'}, dimensions={0}, use_global_device_ids=true | all-gather | bytes 7680 | tf_op jit(solution)/shard_map/all_gather | solution.py:12
  115.0 2.1 convolution_multiply_fusion.3
  118.5 110.6 %while.69 = (s32[]{:T(128)}, f32[384,1024]{1,0:T(8,128)S(1)}, f32[128,1024]{1,0:T(8,128)}, s32[]{:T(128)}, s32[3,8]{0,1:T(8,128)S(1)}, /*index=5*/f32[8,384,128]...) while((s32[]{:T(128)}, f32[384,1024]{1,0:T(8,128)S(1)}, ...), condition=%wide.region_11.12_spmd, body=%wide.region_10.11_spmd.sunk | while | flops 202965152 | bytes 8528964 | solution.py:140
  121.2 14.3 %collective-permute-done.1 = f32[128,1024]{1,0:T(8,128)S(1)} collective-permute-done((f32[128,1024]{1,0:T(8,128)}, f32[128,1024]{1,0:T(8,128)S(1)}, u32[]{:S(2)}, u32[]{:S(2)}) %collective-permute-start.1) | collective-permute-done | bytes 524320 | tf_op jit(solution)/shard_map/while/body/eval_jaxpr/ppermute | solution.py:23
  139.6 13.6 %collective-permute-done.1 = f32[128,1024]{1,0:T(8,128)S(1)} collective-permute-done((f32[128,1024]{1,0:T(8,128)}, f32[128,1024]{1,0:T(8,128)S(1)}, u32[]{:S(2)}, u32[]{:S(2)}) %collective-permute-start.1) | collective-permute-done | bytes 524320 | tf_op jit(solution)/shard_map/while/body/eval_jaxpr/ppermute | solution.py:23
  157.2 12.7 %collective-permute-done.1 = f32[128,1024]{1,0:T(8,128)S(1)} collective-permute-done((f32[128,1024]{1,0:T(8,128)}, f32[128,1024]{1,0:T(8,128)S(1)}, u32[]{:S(2)}, u32[]{:S(2)}) %collective-permute-start.1) | collective-permute-done | bytes 524320 | tf_op jit(solution)/shard_map/while/body/eval_jaxpr/ppermute | solution.py:23
  173.8 11.7 %collective-permute-done.1 = f32[128,1024]{1,0:T(8,128)S(1)} collective-permute-done((f32[128,1024]{1,0:T(8,128)}, f32[128,1024]{1,0:T(8,128)S(1)}, u32[]{:S(2)}, u32[]{:S(2)}) %collective-permute-start.1) | collective-permute-done | bytes 524320 | tf_op jit(solution)/shard_map/while/body/eval_jaxpr/ppermute | solution.py:23
  189.5 10.8 %collective-permute-done.1 = f32[128,1024]{1,0:T(8,128)S(1)} collective-permute-done((f32[128,1024]{1,0:T(8,128)}, f32[128,1024]{1,0:T(8,128)S(1)}, u32[]{:S(2)}, u32[]{:S(2)}) %collective-permute-start.1) | collective-permute-done | bytes 524320 | tf_op jit(solution)/shard_map/while/body/eval_jaxpr/ppermute | solution.py:23
  204.4 9.9 %collective-permute-done.1 = f32[128,1024]{1,0:T(8,128)S(1)} collective-permute-done((f32[128,1024]{1,0:T(8,128)}, f32[128,1024]{1,0:T(8,128)S(1)}, u32[]{:S(2)}, u32[]{:S(2)}) %collective-permute-start.1) | collective-permute-done | bytes 524320 | tf_op jit(solution)/shard_map/while/body/eval_jaxpr/ppermute | solution.py:23
  218.3 9.4 %collective-permute-done.1 = f32[128,1024]{1,0:T(8,128)S(1)} collective-permute-done((f32[128,1024]{1,0:T(8,128)}, f32[128,1024]{1,0:T(8,128)S(1)}, u32[]{:S(2)}, u32[]{:S(2)}) %collective-permute-start.1) | collective-permute-done | bytes 524320 | tf_op jit(solution)/shard_map/while/body/eval_jaxpr/ppermute | solution.py:23
  230.4 11.9 %collective-permute-done.2 = f32[128,1024]{1,0:T(8,128)S(1)} collective-permute-done((f32[128,1024]{1,0:T(8,128)S(1)}, f32[128,1024]{1,0:T(8,128)S(1)}, u32[]{:S(2)}, u32[]{:S(2)}) %collective-permute-start.2) | collective-permute-done | bytes 524320 | tf_op jit(solution)/shard_map/ppermute | solution.py:23
  242.3 27.8 %all-reduce.4.cloned.1.call-done = f32[384,1024]{1,0:T(8,128)} async-done(((f32[384,1024]{1,0:T(8,128)}), f32[384,1024]{1,0:T(8,128)}) %all-reduce.4.cloned.1.call-update) | async-done | bytes 1572880 | tf_op jit(solution)/shard_map/psum | solution.py:142
  270.1 2.7 copy.71
  (197 shorter events, 54.8 us)
Async XLA Ops:
  7.2 5.1 %copy-start.4 = (s32[384]{0:T(512)S(1)}, s32[384]{0:T(512)}, u32[]{:S(2)}) copy-start(s32[384]{0:T(512)} %param.17) | copy-start | bytes 4612
  7.2 262.9 %all-reduce.4.cloned.1.call-start = ((), (), s32[]{:S(2)}) async-start(), calls=%async_computation | async-start | bytes 3145728 | tf_op jit(solution)/shard_map/psum | solution.py:142
  10.6 3.0 %copy-start.3 = (bf16[128,1024]{1,0:T(8,128)(2,1)S(1)}, bf16[128,1024]{1,0:T(8,128)(2,1)}, u32[]{:S(2)}) copy-start(bf16[128,1024]{1,0:T(8,128)(2,1)} %param.15) | copy-start | bytes 786436
  13.6 1.1 copy-start
  14.8 12.5 %collective-permute-start = (bf16[128,1024]{1,0:T(8,128)(2,1)}, bf16[128,1024]{1,0:T(8,128)(2,1)S(1)}, u32[]{:S(2)}, u32[]{:S(2)}) collective-permute-start(bf16[128,1024]{1,0:T(8,128)(2,1)} %get-tuple-element.1277), channel_id=1, source_target_pairs={{0,1},{1,2},{2,3},{3,4},{4,5},{5,6},{6,7},{7,0},{8,9},{9,10},{10,1... | collective-permute-start | bytes 786440 | tf_op jit(solution)/shard_map/while/body/eval_jaxpr/ppermute | solution.py:23
  29.2 10.4 %collective-permute-start = (bf16[128,1024]{1,0:T(8,128)(2,1)}, bf16[128,1024]{1,0:T(8,128)(2,1)S(1)}, u32[]{:S(2)}, u32[]{:S(2)}) collective-permute-start(bf16[128,1024]{1,0:T(8,128)(2,1)} %get-tuple-element.1277), channel_id=1, source_target_pairs={{0,1},{1,2},{2,3},{3,4},{4,5},{5,6},{6,7},{7,0},{8,9},{9,10},{10,1... | collective-permute-start | bytes 786440 | tf_op jit(solution)/shard_map/while/body/eval_jaxpr/ppermute | solution.py:23
  41.7 9.5 %collective-permute-start = (bf16[128,1024]{1,0:T(8,128)(2,1)}, bf16[128,1024]{1,0:T(8,128)(2,1)S(1)}, u32[]{:S(2)}, u32[]{:S(2)}) collective-permute-start(bf16[128,1024]{1,0:T(8,128)(2,1)} %get-tuple-element.1277), channel_id=1, source_target_pairs={{0,1},{1,2},{2,3},{3,4},{4,5},{5,6},{6,7},{7,0},{8,9},{9,10},{10,1... | collective-permute-start | bytes 786440 | tf_op jit(solution)/shard_map/while/body/eval_jaxpr/ppermute | solution.py:23
  53.2 9.3 %collective-permute-start = (bf16[128,1024]{1,0:T(8,128)(2,1)}, bf16[128,1024]{1,0:T(8,128)(2,1)S(1)}, u32[]{:S(2)}, u32[]{:S(2)}) collective-permute-start(bf16[128,1024]{1,0:T(8,128)(2,1)} %get-tuple-element.1277), channel_id=1, source_target_pairs={{0,1},{1,2},{2,3},{3,4},{4,5},{5,6},{6,7},{7,0},{8,9},{9,10},{10,1... | collective-permute-start | bytes 786440 | tf_op jit(solution)/shard_map/while/body/eval_jaxpr/ppermute | solution.py:23
  64.5 9.3 %collective-permute-start = (bf16[128,1024]{1,0:T(8,128)(2,1)}, bf16[128,1024]{1,0:T(8,128)(2,1)S(1)}, u32[]{:S(2)}, u32[]{:S(2)}) collective-permute-start(bf16[128,1024]{1,0:T(8,128)(2,1)} %get-tuple-element.1277), channel_id=1, source_target_pairs={{0,1},{1,2},{2,3},{3,4},{4,5},{5,6},{6,7},{7,0},{8,9},{9,10},{10,1... | collective-permute-start | bytes 786440 | tf_op jit(solution)/shard_map/while/body/eval_jaxpr/ppermute | solution.py:23
  75.9 9.3 %collective-permute-start = (bf16[128,1024]{1,0:T(8,128)(2,1)}, bf16[128,1024]{1,0:T(8,128)(2,1)S(1)}, u32[]{:S(2)}, u32[]{:S(2)}) collective-permute-start(bf16[128,1024]{1,0:T(8,128)(2,1)} %get-tuple-element.1277), channel_id=1, source_target_pairs={{0,1},{1,2},{2,3},{3,4},{4,5},{5,6},{6,7},{7,0},{8,9},{9,10},{10,1... | collective-permute-start | bytes 786440 | tf_op jit(solution)/shard_map/while/body/eval_jaxpr/ppermute | solution.py:23
  87.2 9.3 %collective-permute-start = (bf16[128,1024]{1,0:T(8,128)(2,1)}, bf16[128,1024]{1,0:T(8,128)(2,1)S(1)}, u32[]{:S(2)}, u32[]{:S(2)}) collective-permute-start(bf16[128,1024]{1,0:T(8,128)(2,1)} %get-tuple-element.1277), channel_id=1, source_target_pairs={{0,1},{1,2},{2,3},{3,4},{4,5},{5,6},{6,7},{7,0},{8,9},{9,10},{10,1... | collective-permute-start | bytes 786440 | tf_op jit(solution)/shard_map/while/body/eval_jaxpr/ppermute | solution.py:23
  98.5 16.5 %copy-start.2 = (bf16[8,128,1024]{2,1,0:T(8,128)(2,1)}, bf16[8,128,1024]{2,1,0:T(8,128)(2,1)S(1)}, u32[]{:S(2)}) copy-start(bf16[8,128,1024]{2,1,0:T(8,128)(2,1)S(1)} %get-tuple-element.1351) | copy-start | bytes 6291460
  118.5 17.1 %collective-permute-start.1 = (f32[128,1024]{1,0:T(8,128)}, f32[128,1024]{1,0:T(8,128)S(1)}, u32[]{:S(2)}, u32[]{:S(2)}) collective-permute-start(f32[128,1024]{1,0:T(8,128)} %get-tuple-element.1361), channel_id=1, source_target_pairs={{0,1},{1,2},{2,3},{3,4},{4,5},{5,6},{6,7},{7,0},{8,9},{9,10},{10,1... | collective-permute-start | bytes 1572872 | tf_op jit(solution)/shard_map/while/body/eval_jaxpr/ppermute | solution.py:23
  136.9 16.2 %collective-permute-start.1 = (f32[128,1024]{1,0:T(8,128)}, f32[128,1024]{1,0:T(8,128)S(1)}, u32[]{:S(2)}, u32[]{:S(2)}) collective-permute-start(f32[128,1024]{1,0:T(8,128)} %get-tuple-element.1361), channel_id=1, source_target_pairs={{0,1},{1,2},{2,3},{3,4},{4,5},{5,6},{6,7},{7,0},{8,9},{9,10},{10,1... | collective-permute-start | bytes 1572872 | tf_op jit(solution)/shard_map/while/body/eval_jaxpr/ppermute | solution.py:23
  154.5 15.3 %collective-permute-start.1 = (f32[128,1024]{1,0:T(8,128)}, f32[128,1024]{1,0:T(8,128)S(1)}, u32[]{:S(2)}, u32[]{:S(2)}) collective-permute-start(f32[128,1024]{1,0:T(8,128)} %get-tuple-element.1361), channel_id=1, source_target_pairs={{0,1},{1,2},{2,3},{3,4},{4,5},{5,6},{6,7},{7,0},{8,9},{9,10},{10,1... | collective-permute-start | bytes 1572872 | tf_op jit(solution)/shard_map/while/body/eval_jaxpr/ppermute | solution.py:23
  171.2 14.4 %collective-permute-start.1 = (f32[128,1024]{1,0:T(8,128)}, f32[128,1024]{1,0:T(8,128)S(1)}, u32[]{:S(2)}, u32[]{:S(2)}) collective-permute-start(f32[128,1024]{1,0:T(8,128)} %get-tuple-element.1361), channel_id=1, source_target_pairs={{0,1},{1,2},{2,3},{3,4},{4,5},{5,6},{6,7},{7,0},{8,9},{9,10},{10,1... | collective-permute-start | bytes 1572872 | tf_op jit(solution)/shard_map/while/body/eval_jaxpr/ppermute | solution.py:23
  186.9 13.5 %collective-permute-start.1 = (f32[128,1024]{1,0:T(8,128)}, f32[128,1024]{1,0:T(8,128)S(1)}, u32[]{:S(2)}, u32[]{:S(2)}) collective-permute-start(f32[128,1024]{1,0:T(8,128)} %get-tuple-element.1361), channel_id=1, source_target_pairs={{0,1},{1,2},{2,3},{3,4},{4,5},{5,6},{6,7},{7,0},{8,9},{9,10},{10,1... | collective-permute-start | bytes 1572872 | tf_op jit(solution)/shard_map/while/body/eval_jaxpr/ppermute | solution.py:23
  201.7 12.5 %collective-permute-start.1 = (f32[128,1024]{1,0:T(8,128)}, f32[128,1024]{1,0:T(8,128)S(1)}, u32[]{:S(2)}, u32[]{:S(2)}) collective-permute-start(f32[128,1024]{1,0:T(8,128)} %get-tuple-element.1361), channel_id=1, source_target_pairs={{0,1},{1,2},{2,3},{3,4},{4,5},{5,6},{6,7},{7,0},{8,9},{9,10},{10,1... | collective-permute-start | bytes 1572872 | tf_op jit(solution)/shard_map/while/body/eval_jaxpr/ppermute | solution.py:23
  215.6 12.1 %collective-permute-start.1 = (f32[128,1024]{1,0:T(8,128)}, f32[128,1024]{1,0:T(8,128)S(1)}, u32[]{:S(2)}, u32[]{:S(2)}) collective-permute-start(f32[128,1024]{1,0:T(8,128)} %get-tuple-element.1361), channel_id=1, source_target_pairs={{0,1},{1,2},{2,3},{3,4},{4,5},{5,6},{6,7},{7,0},{8,9},{9,10},{10,1... | collective-permute-start | bytes 1572872 | tf_op jit(solution)/shard_map/while/body/eval_jaxpr/ppermute | solution.py:23
  229.0 1.1 copy-start.1
  229.0 1.4 copy-start.5
  230.4 11.9 %collective-permute-start.2 = (f32[128,1024]{1,0:T(8,128)S(1)}, f32[128,1024]{1,0:T(8,128)S(1)}, u32[]{:S(2)}, u32[]{:S(2)}) collective-permute-start(f32[128,1024]{1,0:T(8,128)S(1)} %copy-done.5), channel_id=1, source_target_pairs={{0,1},{1,2},{2,3},{3,4},{4,5},{5,6},{6,7},{7,0},{8,9},{9,10},{10,1... | collective-permute-start | bytes 1572872 | tf_op jit(solution)/shard_map/ppermute | solution.py:23
Sparse Core Ops, SparseCore 0:
  230.3 39.7 all-reduce.3
where the time goes:
time: 281 us; the launch traced here: 280 us
  waiting for transfers between devices  188 us (67%)
  matrix products  32.2 us (11%)
  local copies, waits for them, and re-layouts  23.6 us (8%)
  blocking collectives  15.5 us (6%)
  between operations  14.1 us (5%)
  starting transfers between devices  3.4 us (1%)
  other arithmetic  3.12 us (1%)
    ppermute x15, waiting for transfers between devices, from_behind(): lax.ppermute(value, axis, [(i, (i + by) % devices) for i in range(devices)])  160 us
    psum x1, waiting for transfers between devices, local(): query_grad = lax.psum(query_part, 'grp')  27.8 us
    all_gather x3, blocking collectives, joined(): everything = jax.tree.map(lambda part: lax.all_gather(part, axis), value)  15.5 us
    dot_general x8, matrix products, gradient_step(): jnp.dot(coef, panel, preferred_element_type=jnp.float32)  11.7 us
    dot_general x8, matrix products, gradient_step(): lax.dot_general(coef, queries, (((0,), (0,)), ((), ())), preferred_elemen...  11.5 us
    dot_general x8, matrix products, panel_scores(): lax.dot_general(queries, panel, (((1,), (1,)), ((), ())), preferred_eleme...  9 us
    unnamed x21, local copies, waits for them, and re-layouts  7.47 us
    dynamic_slice x14, local copies, waits for them, and re-layouts, second_turn(): lax.dynamic_index_in_dim(score_store, turn_index, 0, keepdims=False)  7.44 us
  transfers between devices with their start and end apart: 16, of which 16 were waited for; matrix products, arithmetic and copies ran while one was open for 7% of the time, Pallas kernels for 0%

commit v1 on v0

--- a/solution.py
+++ b/solution.py
@@ -65,6 +65,21 @@
 
 
 def local(queries, docs, compat, positives):
+
+    def _proceed_racks(piece_in):
+        lane_axis = "grp"
+        cores_n = lax.axis_size(lane_axis)
+
+        def fit_matrix_up(val2, later):
+            if later >= cores_n:
+                return val2
+            f_next = lax.ppermute(val2, lane_axis, [(s, s ^ later) for s in range(cores_n)])
+            parts_out = fit_matrix_up(val2 + f_next, 2 * later)
+            return parts_out
+
+        big = fit_matrix_up(piece_in, 1)
+        return big
+
     width = lax.axis_size("dev")
     position = lax.axis_index("dev")
     group_index = lax.axis_index("grp")
@@ -139,7 +154,7 @@
 
     query_part, doc_part = lax.fori_loop(1, width, second_turn, start_carry)
     doc_grad = from_behind(doc_part, "dev", 1)
-    query_grad = lax.psum(query_part, "grp")
+    query_grad = _proceed_racks(query_part)
     return (loss, query_grad, doc_grad)
 
 

time: 281 us -> 266 us (0.947)
  between operations: 14.1 us -> 0.76 us
  local copies, waits for them, and re-layouts: 23.6 us -> 19.5 us
    psum x1 -> x0, waiting for transfers between devices: 27.8 us -> none  [local(): query_grad = lax.psum(query_part, 'grp')]
    ppermute x0 -> x2, waiting for transfers between devices: none -> 22.4 us  [fit_matrix_up(): lax.ppermute(val2, lane_axis, [(s, s ^ later) for s in range(cores_n)])]
    ppermute x15, waiting for transfers between devices: 160 us -> 164 us  [from_behind(): lax.ppermute(value, axis, [(i, (i + by) % devices) for i in range(devices)])]
    unnamed x21 -> x18, local copies, waits for them, and re-layouts: 7.47 us -> 3.37 us
  transfers between devices with their start and end apart: 16 -> 17, of which waited for: 16 -> 17; matrix products, arithmetic and copies ran while one was open for 7% -> 7% of each run, Pallas kernels for 0% -> 0%
where the time goes in v1:
time: 266 us; the launch traced here: 265 us
  waiting for transfers between devices  187 us (70%)
  matrix products  32.2 us (12%)
  local copies, waits for them, and re-layouts  19.5 us (7%)
  blocking collectives  15.5 us (6%)
  other arithmetic  4.81 us (2%)
  starting transfers between devices  4.5 us (2%)
    ppermute x15, waiting for transfers between devices, from_behind(): lax.ppermute(value, axis, [(i, (i + by) % devices) for i in range(devices)])  164 us
    ppermute x2, waiting for transfers between devices, fit_matrix_up(): lax.ppermute(val2, lane_axis, [(s, s ^ later) for s in range(cores_n)])  22.4 us
    all_gather x3, blocking collectives, joined(): everything = jax.tree.map(lambda part: lax.all_gather(part, axis), value)  15.5 us
    dot_general x8, matrix products, gradient_step(): jnp.dot(coef, panel, preferred_element_type=jnp.float32)  11.7 us
    dot_general x8, matrix products, gradient_step(): lax.dot_general(coef, queries, (((0,), (0,)), ((), ())), preferred_elemen...  11.5 us
    dot_general x8, matrix products, panel_scores(): lax.dot_general(queries, panel, (((1,), (1,)), ((), ())), preferred_eleme...  9 us
    dynamic_slice x14, local copies, waits for them, and re-layouts, second_turn(): lax.dynamic_index_in_dim(score_store, turn_index, 0, keepdims=False)  7.44 us
  transfers between devices with their start and end apart: 17, of which 17 were waited for; matrix products, arithmetic and copies ran while one was open for 7% of the time, Pallas kernels for 0%

profile of v1, /device:TPU:0, one launch (start us, length us, event | category | flops | bytes accessed | tf_op | source)
XLA Modules:
  0.0 264.9 jit_solution(1222197388995258729)
XLA Ops:
  8.2 83.8 %while.67 = (s32[]{:T(128)}, bf16[128,1024]{1,0:T(8,128)(2,1)}, bf16[8,128,1024]{2,1,0:T(8,128)(2,1)S(1)}, f32[8,384,128]{1,2,0:T(8,128)}, f32[384]{0:T(512)S(1)...) while((s32[]{:T(128)}, bf16[128,1024]{1,0:T(8,128)(2,1)}, ...), condition=%wide.region_7.8_spmd, body=%wide.region_3.7_spmd.sunk | while | flops 101106560 | bytes 3962444 | solution.py:137
  8.2 2.9 %collective-permute-start = (bf16[128,1024]{1,0:T(8,128)(2,1)}, bf16[128,1024]{1,0:T(8,128)(2,1)S(1)}, u32[]{:S(2)}, u32[]{:S(2)}) collective-permute-start(bf16[128,1024]{1,0:T(8,128)(2,1)} %get-tuple-element.1277), channel_id=1, source_target_pairs={{0,1},{1,2},{2,3},{3,4},{4,5},{5,6},{6,7},{7,0},{8,9},{9,10},{10,1... | collective-permute-start | bytes 786440 | tf_op jit(solution)/shard_map/while/body/eval_jaxpr/ppermute | solution.py:23
  11.2 9.5 %collective-permute-done = bf16[128,1024]{1,0:T(8,128)(2,1)S(1)} collective-permute-done((bf16[128,1024]{1,0:T(8,128)(2,1)}, bf16[128,1024]{1,0:T(8,128)(2,1)S(1)}, u32[]{:S(2)}, u32[]{:S(2)}) %collective-permute-start) | collective-permute-done | bytes 262176 | tf_op jit(solution)/shard_map/while/body/eval_jaxpr/ppermute | solution.py:23
  22.9 10.2 %collective-permute-done = bf16[128,1024]{1,0:T(8,128)(2,1)S(1)} collective-permute-done((bf16[128,1024]{1,0:T(8,128)(2,1)}, bf16[128,1024]{1,0:T(8,128)(2,1)S(1)}, u32[]{:S(2)}, u32[]{:S(2)}) %collective-permute-start) | collective-permute-done | bytes 262176 | tf_op jit(solution)/shard_map/while/body/eval_jaxpr/ppermute | solution.py:23
  35.3 9.3 %collective-permute-done = bf16[128,1024]{1,0:T(8,128)(2,1)S(1)} collective-permute-done((bf16[128,1024]{1,0:T(8,128)(2,1)}, bf16[128,1024]{1,0:T(8,128)(2,1)S(1)}, u32[]{:S(2)}, u32[]{:S(2)}) %collective-permute-start) | collective-permute-done | bytes 262176 | tf_op jit(solution)/shard_map/while/body/eval_jaxpr/ppermute | solution.py:23
  46.9 9.1 %collective-permute-done = bf16[128,1024]{1,0:T(8,128)(2,1)S(1)} collective-permute-done((bf16[128,1024]{1,0:T(8,128)(2,1)}, bf16[128,1024]{1,0:T(8,128)(2,1)S(1)}, u32[]{:S(2)}, u32[]{:S(2)}) %collective-permute-start) | collective-permute-done | bytes 262176 | tf_op jit(solution)/shard_map/while/body/eval_jaxpr/ppermute | solution.py:23
  58.2 9.1 %collective-permute-done = bf16[128,1024]{1,0:T(8,128)(2,1)S(1)} collective-permute-done((bf16[128,1024]{1,0:T(8,128)(2,1)}, bf16[128,1024]{1,0:T(8,128)(2,1)S(1)}, u32[]{:S(2)}, u32[]{:S(2)}) %collective-permute-start) | collective-permute-done | bytes 262176 | tf_op jit(solution)/shard_map/while/body/eval_jaxpr/ppermute | solution.py:23
  69.5 9.1 %collective-permute-done = bf16[128,1024]{1,0:T(8,128)(2,1)S(1)} collective-permute-done((bf16[128,1024]{1,0:T(8,128)(2,1)}, bf16[128,1024]{1,0:T(8,128)(2,1)S(1)}, u32[]{:S(2)}, u32[]{:S(2)}) %collective-permute-start) | collective-permute-done | bytes 262176 | tf_op jit(solution)/shard_map/while/body/eval_jaxpr/ppermute | solution.py:23
  80.9 9.1 %collective-permute-done = bf16[128,1024]{1,0:T(8,128)(2,1)S(1)} collective-permute-done((bf16[128,1024]{1,0:T(8,128)(2,1)}, bf16[128,1024]{1,0:T(8,128)(2,1)S(1)}, u32[]{:S(2)}, u32[]{:S(2)}) %collective-permute-start) | collective-permute-done | bytes 262176 | tf_op jit(solution)/shard_map/while/body/eval_jaxpr/ppermute | solution.py:23
  92.0 5.2 %all-gather.5 = f32[4,1,384]{2,1,0:T(1,128)S(1)} all-gather(f32[1,1,384]{2,1,0:T(1,128)S(1)} %reshape.269), channel_id=4, replica_groups=mesh['grp'=4,'dev'=8] {'grp'}, dimensions={0}, use_global_device_ids=true | all-gather | bytes 7680 | tf_op jit(solution)/shard_map/all_gather | solution.py:12
  97.2 5.2 %all-gather.4 = f32[4,1,384]{2,1,0:T(1,128)S(1)} all-gather(f32[1,1,384]{2,1,0:T(1,128)S(1)} %reshape.267), channel_id=3, replica_groups=mesh['grp'=4,'dev'=8] {'grp'}, dimensions={0}, use_global_device_ids=true | all-gather | bytes 7680 | tf_op jit(solution)/shard_map/all_gather | solution.py:12
  102.3 5.2 %all-gather.3 = f32[4,1,384]{2,1,0:T(1,128)S(1)} all-gather(f32[1,1,384]{2,1,0:T(1,128)S(1)} %reshape.265), channel_id=2, replica_groups=mesh['grp'=4,'dev'=8] {'grp'}, dimensions={0}, use_global_device_ids=true | all-gather | bytes 7680 | tf_op jit(solution)/shard_map/all_gather | solution.py:12
  108.4 2.1 convolution_multiply_fusion.3
  111.9 110.6 %while.69 = (s32[]{:T(128)}, f32[384,1024]{1,0:T(8,128)S(1)}, f32[128,1024]{1,0:T(8,128)}, s32[]{:T(128)}, s32[3,8]{0,1:T(8,128)S(1)}, /*index=5*/f32[8,384,128]...) while((s32[]{:T(128)}, f32[384,1024]{1,0:T(8,128)S(1)}, ...), condition=%wide.region_11.12_spmd, body=%wide.region_10.11_spmd.sunk | while | flops 202965152 | bytes 8528964 | solution.py:155
  114.7 14.3 %collective-permute-done.1 = f32[128,1024]{1,0:T(8,128)S(1)} collective-permute-done((f32[128,1024]{1,0:T(8,128)}, f32[128,1024]{1,0:T(8,128)S(1)}, u32[]{:S(2)}, u32[]{:S(2)}) %collective-permute-start.1) | collective-permute-done | bytes 524320 | tf_op jit(solution)/shard_map/while/body/eval_jaxpr/ppermute | solution.py:23
  133.0 13.6 %collective-permute-done.1 = f32[128,1024]{1,0:T(8,128)S(1)} collective-permute-done((f32[128,1024]{1,0:T(8,128)}, f32[128,1024]{1,0:T(8,128)S(1)}, u32[]{:S(2)}, u32[]{:S(2)}) %collective-permute-start.1) | collective-permute-done | bytes 524320 | tf_op jit(solution)/shard_map/while/body/eval_jaxpr/ppermute | solution.py:23
  150.6 12.7 %collective-permute-done.1 = f32[128,1024]{1,0:T(8,128)S(1)} collective-permute-done((f32[128,1024]{1,0:T(8,128)}, f32[128,1024]{1,0:T(8,128)S(1)}, u32[]{:S(2)}, u32[]{:S(2)}) %collective-permute-start.1) | collective-permute-done | bytes 524320 | tf_op jit(solution)/shard_map/while/body/eval_jaxpr/ppermute | solution.py:23
  167.2 11.7 %collective-permute-done.1 = f32[128,1024]{1,0:T(8,128)S(1)} collective-permute-done((f32[128,1024]{1,0:T(8,128)}, f32[128,1024]{1,0:T(8,128)S(1)}, u32[]{:S(2)}, u32[]{:S(2)}) %collective-permute-start.1) | collective-permute-done | bytes 524320 | tf_op jit(solution)/shard_map/while/body/eval_jaxpr/ppermute | solution.py:23
  183.0 10.8 %collective-permute-done.1 = f32[128,1024]{1,0:T(8,128)S(1)} collective-permute-done((f32[128,1024]{1,0:T(8,128)}, f32[128,1024]{1,0:T(8,128)S(1)}, u32[]{:S(2)}, u32[]{:S(2)}) %collective-permute-start.1) | collective-permute-done | bytes 524320 | tf_op jit(solution)/shard_map/while/body/eval_jaxpr/ppermute | solution.py:23
  197.8 9.9 %collective-permute-done.1 = f32[128,1024]{1,0:T(8,128)S(1)} collective-permute-done((f32[128,1024]{1,0:T(8,128)}, f32[128,1024]{1,0:T(8,128)S(1)}, u32[]{:S(2)}, u32[]{:S(2)}) %collective-permute-start.1) | collective-permute-done | bytes 524320 | tf_op jit(solution)/shard_map/while/body/eval_jaxpr/ppermute | solution.py:23
  211.7 9.4 %collective-permute-done.1 = f32[128,1024]{1,0:T(8,128)S(1)} collective-permute-done((f32[128,1024]{1,0:T(8,128)}, f32[128,1024]{1,0:T(8,128)S(1)}, u32[]{:S(2)}, u32[]{:S(2)}) %collective-permute-start.1) | collective-permute-done | bytes 524320 | tf_op jit(solution)/shard_map/while/body/eval_jaxpr/ppermute | solution.py:23
  222.5 3.4 %collective-permute-done.2 = f32[384,1024]{1,0:T(8,128)S(1)} collective-permute-done((f32[384,1024]{1,0:T(8,128)S(1)}, f32[384,1024]{1,0:T(8,128)S(1)}, u32[]{:S(2)}, u32[]{:S(2)}) %collective-permute-start.2) | collective-permute-done | bytes 1572896 | tf_op jit(solution)/shard_map/ppermute | solution.py:76
  227.3 16.4 %collective-permute-done.4 = f32[128,1024]{1,0:T(8,128)S(1)} collective-permute-done((f32[128,1024]{1,0:T(8,128)S(1)}, f32[128,1024]{1,0:T(8,128)S(1)}, u32[]{:S(2)}, u32[]{:S(2)}) %collective-permute-start.4) | collective-permute-done | bytes 524320 | tf_op jit(solution)/shard_map/ppermute | solution.py:23
  243.7 19.0 %collective-permute-done.3 = f32[384,1024]{1,0:T(8,128)S(1)} collective-permute-done((f32[384,1024]{1,0:T(8,128)S(1)}, f32[384,1024]{1,0:T(8,128)S(1)}, u32[]{:S(2)}, u32[]{:S(2)}) %collective-permute-start.3) | collective-permute-done | bytes 1572896 | tf_op jit(solution)/shard_map/ppermute | solution.py:76
  (197 shorter events, 56.2 us)
Async XLA Ops:
  0.6 5.0 %copy-start.3 = (s32[384]{0:T(512)S(1)}, s32[384]{0:T(512)}, u32[]{:S(2)}) copy-start(s32[384]{0:T(512)} %param.17) | copy-start | bytes 4612
  4.0 3.0 %copy-start.2 = (bf16[128,1024]{1,0:T(8,128)(2,1)S(1)}, bf16[128,1024]{1,0:T(8,128)(2,1)}, u32[]{:S(2)}) copy-start(bf16[128,1024]{1,0:T(8,128)(2,1)} %param.15) | copy-start | bytes 786436
  7.0 1.1 copy-start
  8.2 12.5 %collective-permute-start = (bf16[128,1024]{1,0:T(8,128)(2,1)}, bf16[128,1024]{1,0:T(8,128)(2,1)S(1)}, u32[]{:S(2)}, u32[]{:S(2)}) collective-permute-start(bf16[128,1024]{1,0:T(8,128)(2,1)} %get-tuple-element.1277), channel_id=1, source_target_pairs={{0,1},{1,2},{2,3},{3,4},{4,5},{5,6},{6,7},{7,0},{8,9},{9,10},{10,1... | collective-permute-start | bytes 786440 | tf_op jit(solution)/shard_map/while/body/eval_jaxpr/ppermute | solution.py:23
  22.7 10.5 %collective-permute-start = (bf16[128,1024]{1,0:T(8,128)(2,1)}, bf16[128,1024]{1,0:T(8,128)(2,1)S(1)}, u32[]{:S(2)}, u32[]{:S(2)}) collective-permute-start(bf16[128,1024]{1,0:T(8,128)(2,1)} %get-tuple-element.1277), channel_id=1, source_target_pairs={{0,1},{1,2},{2,3},{3,4},{4,5},{5,6},{6,7},{7,0},{8,9},{9,10},{10,1... | collective-permute-start | bytes 786440 | tf_op jit(solution)/shard_map/while/body/eval_jaxpr/ppermute | solution.py:23
  35.1 9.5 %collective-permute-start = (bf16[128,1024]{1,0:T(8,128)(2,1)}, bf16[128,1024]{1,0:T(8,128)(2,1)S(1)}, u32[]{:S(2)}, u32[]{:S(2)}) collective-permute-start(bf16[128,1024]{1,0:T(8,128)(2,1)} %get-tuple-element.1277), channel_id=1, source_target_pairs={{0,1},{1,2},{2,3},{3,4},{4,5},{5,6},{6,7},{7,0},{8,9},{9,10},{10,1... | collective-permute-start | bytes 786440 | tf_op jit(solution)/shard_map/while/body/eval_jaxpr/ppermute | solution.py:23
  46.6 9.3 %collective-permute-start = (bf16[128,1024]{1,0:T(8,128)(2,1)}, bf16[128,1024]{1,0:T(8,128)(2,1)S(1)}, u32[]{:S(2)}, u32[]{:S(2)}) collective-permute-start(bf16[128,1024]{1,0:T(8,128)(2,1)} %get-tuple-element.1277), channel_id=1, source_target_pairs={{0,1},{1,2},{2,3},{3,4},{4,5},{5,6},{6,7},{7,0},{8,9},{9,10},{10,1... | collective-permute-start | bytes 786440 | tf_op jit(solution)/shard_map/while/body/eval_jaxpr/ppermute | solution.py:23
  58.0 9.3 %collective-permute-start = (bf16[128,1024]{1,0:T(8,128)(2,1)}, bf16[128,1024]{1,0:T(8,128)(2,1)S(1)}, u32[]{:S(2)}, u32[]{:S(2)}) collective-permute-start(bf16[128,1024]{1,0:T(8,128)(2,1)} %get-tuple-element.1277), channel_id=1, source_target_pairs={{0,1},{1,2},{2,3},{3,4},{4,5},{5,6},{6,7},{7,0},{8,9},{9,10},{10,1... | collective-permute-start | bytes 786440 | tf_op jit(solution)/shard_map/while/body/eval_jaxpr/ppermute | solution.py:23
  69.3 9.3 %collective-permute-start = (bf16[128,1024]{1,0:T(8,128)(2,1)}, bf16[128,1024]{1,0:T(8,128)(2,1)S(1)}, u32[]{:S(2)}, u32[]{:S(2)}) collective-permute-start(bf16[128,1024]{1,0:T(8,128)(2,1)} %get-tuple-element.1277), channel_id=1, source_target_pairs={{0,1},{1,2},{2,3},{3,4},{4,5},{5,6},{6,7},{7,0},{8,9},{9,10},{10,1... | collective-permute-start | bytes 786440 | tf_op jit(solution)/shard_map/while/body/eval_jaxpr/ppermute | solution.py:23
  80.6 9.3 %collective-permute-start = (bf16[128,1024]{1,0:T(8,128)(2,1)}, bf16[128,1024]{1,0:T(8,128)(2,1)S(1)}, u32[]{:S(2)}, u32[]{:S(2)}) collective-permute-start(bf16[128,1024]{1,0:T(8,128)(2,1)} %get-tuple-element.1277), channel_id=1, source_target_pairs={{0,1},{1,2},{2,3},{3,4},{4,5},{5,6},{6,7},{7,0},{8,9},{9,10},{10,1... | collective-permute-start | bytes 786440 | tf_op jit(solution)/shard_map/while/body/eval_jaxpr/ppermute | solution.py:23
  92.0 16.5 %copy-start.1 = (bf16[8,128,1024]{2,1,0:T(8,128)(2,1)}, bf16[8,128,1024]{2,1,0:T(8,128)(2,1)S(1)}, u32[]{:S(2)}) copy-start(bf16[8,128,1024]{2,1,0:T(8,128)(2,1)S(1)} %get-tuple-element.1351) | copy-start | bytes 6291460
  111.9 17.1 %collective-permute-start.1 = (f32[128,1024]{1,0:T(8,128)}, f32[128,1024]{1,0:T(8,128)S(1)}, u32[]{:S(2)}, u32[]{:S(2)}) collective-permute-start(f32[128,1024]{1,0:T(8,128)} %get-tuple-element.1361), channel_id=1, source_target_pairs={{0,1},{1,2},{2,3},{3,4},{4,5},{5,6},{6,7},{7,0},{8,9},{9,10},{10,1... | collective-permute-start | bytes 1572872 | tf_op jit(solution)/shard_map/while/body/eval_jaxpr/ppermute | solution.py:23
  130.3 16.2 %collective-permute-start.1 = (f32[128,1024]{1,0:T(8,128)}, f32[128,1024]{1,0:T(8,128)S(1)}, u32[]{:S(2)}, u32[]{:S(2)}) collective-permute-start(f32[128,1024]{1,0:T(8,128)} %get-tuple-element.1361), channel_id=1, source_target_pairs={{0,1},{1,2},{2,3},{3,4},{4,5},{5,6},{6,7},{7,0},{8,9},{9,10},{10,1... | collective-permute-start | bytes 1572872 | tf_op jit(solution)/shard_map/while/body/eval_jaxpr/ppermute | solution.py:23
  147.9 15.3 %collective-permute-start.1 = (f32[128,1024]{1,0:T(8,128)}, f32[128,1024]{1,0:T(8,128)S(1)}, u32[]{:S(2)}, u32[]{:S(2)}) collective-permute-start(f32[128,1024]{1,0:T(8,128)} %get-tuple-element.1361), channel_id=1, source_target_pairs={{0,1},{1,2},{2,3},{3,4},{4,5},{5,6},{6,7},{7,0},{8,9},{9,10},{10,1... | collective-permute-start | bytes 1572872 | tf_op jit(solution)/shard_map/while/body/eval_jaxpr/ppermute | solution.py:23
  164.6 14.4 %collective-permute-start.1 = (f32[128,1024]{1,0:T(8,128)}, f32[128,1024]{1,0:T(8,128)S(1)}, u32[]{:S(2)}, u32[]{:S(2)}) collective-permute-start(f32[128,1024]{1,0:T(8,128)} %get-tuple-element.1361), channel_id=1, source_target_pairs={{0,1},{1,2},{2,3},{3,4},{4,5},{5,6},{6,7},{7,0},{8,9},{9,10},{10,1... | collective-permute-start | bytes 1572872 | tf_op jit(solution)/shard_map/while/body/eval_jaxpr/ppermute | solution.py:23
  180.3 13.5 %collective-permute-start.1 = (f32[128,1024]{1,0:T(8,128)}, f32[128,1024]{1,0:T(8,128)S(1)}, u32[]{:S(2)}, u32[]{:S(2)}) collective-permute-start(f32[128,1024]{1,0:T(8,128)} %get-tuple-element.1361), channel_id=1, source_target_pairs={{0,1},{1,2},{2,3},{3,4},{4,5},{5,6},{6,7},{7,0},{8,9},{9,10},{10,1... | collective-permute-start | bytes 1572872 | tf_op jit(solution)/shard_map/while/body/eval_jaxpr/ppermute | solution.py:23
  195.1 12.5 %collective-permute-start.1 = (f32[128,1024]{1,0:T(8,128)}, f32[128,1024]{1,0:T(8,128)S(1)}, u32[]{:S(2)}, u32[]{:S(2)}) collective-permute-start(f32[128,1024]{1,0:T(8,128)} %get-tuple-element.1361), channel_id=1, source_target_pairs={{0,1},{1,2},{2,3},{3,4},{4,5},{5,6},{6,7},{7,0},{8,9},{9,10},{10,1... | collective-permute-start | bytes 1572872 | tf_op jit(solution)/shard_map/while/body/eval_jaxpr/ppermute | solution.py:23
  209.0 12.1 %collective-permute-start.1 = (f32[128,1024]{1,0:T(8,128)}, f32[128,1024]{1,0:T(8,128)S(1)}, u32[]{:S(2)}, u32[]{:S(2)}) collective-permute-start(f32[128,1024]{1,0:T(8,128)} %get-tuple-element.1361), channel_id=1, source_target_pairs={{0,1},{1,2},{2,3},{3,4},{4,5},{5,6},{6,7},{7,0},{8,9},{9,10},{10,1... | collective-permute-start | bytes 1572872 | tf_op jit(solution)/shard_map/while/body/eval_jaxpr/ppermute | solution.py:23
  222.5 4.8 %copy-start.4 = (f32[128,1024]{1,0:T(8,128)S(1)}, f32[128,1024]{1,0:T(8,128)}, u32[]{:S(2)}) copy-start(f32[128,1024]{1,0:T(8,128)} %get-tuple-element.938) | copy-start | bytes 1572868
  222.5 3.4 %collective-permute-start.2 = (f32[384,1024]{1,0:T(8,128)S(1)}, f32[384,1024]{1,0:T(8,128)S(1)}, u32[]{:S(2)}, u32[]{:S(2)}) collective-permute-start(f32[384,1024]{1,0:T(8,128)S(1)} %get-tuple-element.937), channel_id=1, source_target_pairs={{0,8},{8,0},{16,24},{24,16},{1,9},{9,1},{17,25},{25,17},{2,10},{10... | collective-permute-start | bytes 4718600 | tf_op jit(solution)/shard_map/ppermute | solution.py:76
  226.2 36.5 %collective-permute-start.3 = (f32[384,1024]{1,0:T(8,128)S(1)}, f32[384,1024]{1,0:T(8,128)S(1)}, u32[]{:S(2)}, u32[]{:S(2)}) collective-permute-start(f32[384,1024]{1,0:T(8,128)S(1)} %add.366), channel_id=1, source_target_pairs={{0,16},{8,24},{16,0},{24,8},{1,17},{9,25},{17,1},{25,9},{2,18},{10... | collective-permute-start | bytes 4718600 | tf_op jit(solution)/shard_map/ppermute | solution.py:76
  227.3 16.4 %collective-permute-start.4 = (f32[128,1024]{1,0:T(8,128)S(1)}, f32[128,1024]{1,0:T(8,128)S(1)}, u32[]{:S(2)}, u32[]{:S(2)}) collective-permute-start(f32[128,1024]{1,0:T(8,128)S(1)} %copy-done.4), channel_id=1, source_target_pairs={{0,1},{1,2},{2,3},{3,4},{4,5},{5,6},{6,7},{7,0},{8,9},{9,10},{10,1... | collective-permute-start | bytes 1572872 | tf_op jit(solution)/shard_map/ppermute | solution.py:23
